TPU v7x, 768 devices: a whole 4x8x12 slice. The times are simulated.
768 devices in a mesh: user: 32 (over x, y_hi, core), item: 24 (over y_lo, z).
Axes of the slice: x: 4, y: 8 (y_hi: 4, y_lo: 2; y = y_hi * 2 + y_lo), z: 12, core: 2. Of those that a mesh axis runs over, the one named last changes fastest.
Arguments:
- tile_index: int32 [32, 24, 48], P('user', 'item'), may hold values from -1 to 1535, as said below
- tile_values: bfloat16 [32, 24, 48, 128, 128], P('user', 'item'), may hold values from 10 to 1000
- w_init: float32 [64, 196608], P(None, ('user', 'item')), may hold values from 0.01 to 20, as said below
- h_init: float32 [64, 98304], P(None, ('item', 'user')), may hold values from 0.0001 to 1, as said below
Outputs:
- w_new: float32 [64, 196608], P(None, ('user', 'item'))
- h_new: float32 [64, 98304], P(None, ('item', 'user'))
Inputs may be any that keep to these rules, and one draw needn't show every extreme that they name: `tile_index`: in each block the slots holding a tile come first and the rest hold -1; the tiles of one block are distinct, no two of them among the same 32 consecutive tile numbers; every block holds at least 12 tiles; every slot holds a tile in some block. `w_init`: all entries are positive. `h_init`: all entries are positive.
All inputs are finite; a program needn't handle non-finite values.
Results may differ from a plain program's by a relative error of at most 0.0038.
Values may be sent and summed in bfloat16 or wider, within the bound.
A program may use at most 32 MiB of HBM per device.

v0:
```python
import jax
import jax.numpy as jnp
from jax import lax
from jax.sharding import PartitionSpec as P

TILE = 128
USER_TILES = 48
ITEM_TILES = 32


floor_value = 0.0001


def hals_sweep(factor, cross, gram):

    def update(column, current):
        gram_row = lax.dynamic_index_in_dim(gram, column, 0, keepdims=False)
        pivot = lax.dynamic_index_in_dim(gram_row, column, 0, keepdims=False)
        old_row = lax.dynamic_index_in_dim(current, column, 0, keepdims=False)
        cross_row = lax.dynamic_index_in_dim(cross, column, 0, keepdims=False)
        fitted = jnp.dot(gram_row, current, precision=lax.Precision.HIGHEST)
        new_row = jnp.maximum(old_row + (cross_row - fitted) / pivot, floor_value)
        return lax.dynamic_update_index_in_dim(current, new_row, column, 0)

    return lax.fori_loop(0, factor.shape[0], update, factor)


def shards(tile_index, tile_values, w_init, h_init):
    rank_size = w_init.shape[0]
    slot_ids = tile_index[0, 0]
    values = tile_values[0, 0]
    weight = (slot_ids >= 0).astype(jnp.float32)
    clipped = jnp.maximum(slot_ids, 0)
    tile_rows = clipped // ITEM_TILES
    tile_cols = clipped % ITEM_TILES
    h_half = h_init.astype(jnp.bfloat16)
    h_block = lax.all_gather(h_half, "user", axis=1, tiled=True)
    gram_h = lax.psum(
        jnp.dot(h_half, h_half.T, preferred_element_type=jnp.float32), ("user", "item")
    )
    chosen = jnp.take(h_block.reshape(rank_size, ITEM_TILES, TILE), tile_cols, axis=1)
    products = (
        jnp.einsum("ksi,sui->sku", chosen, values, preferred_element_type=jnp.float32)
        * weight[:, None, None]
    )
    summed = jax.ops.segment_sum(products, tile_rows, num_segments=USER_TILES)
    partial_value = jnp.transpose(summed, (1, 0, 2)).reshape(rank_size, USER_TILES * TILE)
    cross_w = lax.psum_scatter(partial_value, "item", scatter_dimension=1, tiled=True)
    w_new = hals_sweep(w_init, cross_w, gram_h)
    w_half = w_new.astype(jnp.bfloat16)
    w_block = lax.all_gather(w_half, "item", axis=1, tiled=True)
    gram_w = lax.psum(
        jnp.dot(w_half, w_half.T, preferred_element_type=jnp.float32), ("user", "item")
    )
    chosen_rows = jnp.take(w_block.reshape(rank_size, USER_TILES, TILE), tile_rows, axis=1)
    products_h = (
        jnp.einsum("ksu,sui->ski", chosen_rows, values, preferred_element_type=jnp.float32)
        * weight[:, None, None]
    )
    summed_h = jax.ops.segment_sum(products_h, tile_cols, num_segments=ITEM_TILES)
    partial_h = jnp.transpose(summed_h, (1, 0, 2)).reshape(rank_size, ITEM_TILES * TILE)
    cross_h = lax.psum_scatter(partial_h, "user", scatter_dimension=1, tiled=True)
    h_new = hals_sweep(h_init, cross_h, gram_w)
    return (w_new, h_new)


def solution(mesh):
    in_specs = (
        P("user", "item", None),
        P("user", "item", None, None, None),
        P(None, ("user", "item")),
        P(None, ("item", "user")),
    )
    out_specs = (P(None, ("user", "item")), P(None, ("item", "user")))
    return jax.shard_map(shards, mesh=mesh, in_specs=in_specs, out_specs=out_specs, check_vma=False)
```

profile of v0, /device:TPU:1, one launch (start us, length us, event | category | flops | bytes accessed | tf_op | source)
XLA Modules:
  0.0 636.0 jit_solution(4491285089030977794)
XLA Ops:
  10.1 50.6 %all_gather.6 = bf16[64,4096]{1,0:T(8,128)(2,1)S(1)} all-gather(bf16[64,128]{1,0:T(8,128)(2,1)S(1)} %convert_element_type.16), channel_id=1, replica_groups=mesh['user'=32,'item'=24] {'user'}, dimensions={1}, use_global_device_ids=true | all-gather | bytes 540672 | tf_op jit(solution)/shard_map/all_gather | solution.py:37
  61.6 2.3 fusion.17
  64.1 5.4 scatter_fusion
  71.0 113.2 %psum.14 = f32[64,64]{1,0:T(8,128)S(1)} all-reduce(f32[64,64]{1,0:T(8,128)S(1)} %fusion.39), channel_id=1, replica_groups=mesh['user'=32,'item'=24] {'user','item'}, use_global_device_ids=true, to_apply=%region_0.1 | all-reduce | flops 4096 | bytes 32768 | tf_op jit(solution)/shard_map/psum | solution.py:38
  184.2 138.2 %while.32 = (s32[]{:T(128)}, f32[64,256]{1,0:T(8,128)S(1)}, f32[64,256]{1,0:T(8,128)}, f32[64,64]{1,0:T(8,128)S(1)}, s32[]{:T(128)}, /*index=5*/s32[]{:T(128)}, s32[]{:T(128)}) while((s32[]{:T(128)}, f32[64,256]{1,0:T(8,128)S(1)}, f32[64,256]{1,0:T(8,128)}, f32[64,64]{1,0:T(8,128)S(1)}, s32[]{:T(128)}, /*index=5*/s32[]{:T(128)}, ...), condition=%wide.region_4.5_spmd, body=%wide.region_3.4_spmd.sunk | while | flops 197635 | bytes 77433 | solution.py:25
  322.4 39.3 %all_gather.7 = bf16[64,6144]{1,0:T(8,128)(2,1)S(1)} all-gather(bf16[64,256]{1,0:T(8,128)(2,1)S(1)} %convert_element_type.19), channel_id=1, replica_groups=mesh['user'=32,'item'=24] {'item'}, dimensions={1}, use_global_device_ids=true | all-gather | bytes 819200 | tf_op jit(solution)/shard_map/all_gather | solution.py:51
  362.7 1.8 fusion.20
  364.6 5.4 scatter_fusion.1
  371.2 115.2 %psum.15 = f32[64,64]{1,0:T(8,128)S(1)} all-reduce(f32[64,64]{1,0:T(8,128)S(1)} %fusion.40), channel_id=1, replica_groups=mesh['user'=32,'item'=24] {'user','item'}, use_global_device_ids=true, to_apply=%region_5.6 | all-reduce | flops 4096 | bytes 32768 | tf_op jit(solution)/shard_map/psum | solution.py:52
  486.4 142.1 %while.33 = (s32[]{:T(128)}, f32[64,128]{1,0:T(8,128)S(1)}, f32[64,128]{1,0:T(8,128)}, f32[64,64]{1,0:T(8,128)S(1)}, s32[]{:T(128)}, /*index=5*/s32[]{:T(128)}, s32[]{:T(128)}) while((s32[]{:T(128)}, f32[64,128]{1,0:T(8,128)S(1)}, f32[64,128]{1,0:T(8,128)}, f32[64,64]{1,0:T(8,128)S(1)}, s32[]{:T(128)}, /*index=5*/s32[]{:T(128)}, ...), condition=%wide.region_9.10_spmd, body=%wide.region_8.9_spmd.sunk | while | flops 98819 | bytes 37485 | solution.py:25
  487.0 1.5 fusion.64
  489.3 1.5 fusion.64
  491.5 1.5 fusion.64
  493.7 1.5 fusion.64
  495.9 1.5 fusion.64
  498.1 1.5 fusion.64
  500.4 1.5 fusion.64
  502.6 1.5 fusion.64
  504.8 1.5 fusion.64
  507.0 1.5 fusion.64
  509.2 1.5 fusion.64
  511.4 1.5 fusion.64
  513.7 1.5 fusion.64
  515.9 1.5 fusion.64
  518.1 1.5 fusion.64
  520.3 1.5 fusion.64
  522.5 1.5 fusion.64
  524.7 1.5 fusion.64
  527.0 1.5 fusion.64
  529.2 1.5 fusion.64
  531.4 1.5 fusion.64
  533.6 1.5 fusion.64
  535.9 1.5 fusion.64
  538.1 1.5 fusion.64
  540.3 1.5 fusion.64
  542.6 1.5 fusion.64
  544.8 1.5 fusion.64
  547.0 1.5 fusion.64
  549.2 1.5 fusion.64
  551.4 1.5 fusion.64
  553.7 1.5 fusion.64
  555.9 1.5 fusion.64
  558.1 1.5 fusion.64
  560.3 1.5 fusion.64
  562.6 1.5 fusion.64
  564.8 1.5 fusion.64
  567.0 1.5 fusion.64
  569.2 1.5 fusion.64
  571.5 1.5 fusion.64
  573.7 1.5 fusion.64
  575.9 1.5 fusion.64
  578.1 1.5 fusion.64
  580.4 1.5 fusion.64
  582.6 1.5 fusion.64
  584.8 1.5 fusion.64
  587.0 1.5 fusion.64
  589.3 1.5 fusion.64
  591.5 1.5 fusion.64
  598.2 1.5 fusion.64
  600.4 1.5 fusion.64
  602.6 1.5 fusion.64
  604.8 1.5 fusion.64
  607.0 1.5 fusion.64
  609.2 1.5 fusion.64
  (490 shorter events, 203.9 us)
Async XLA Ops:
  7.2 54.4 %copy-start = (bf16[1,1,48,128,128]{4,3,2,1,0:T(8,128)(2,1)S(1)}, bf16[1,1,48,128,128]{4,3,2,1,0:T(8,128)(2,1)}, u32[]{:S(2)}) copy-start(bf16[1,1,48,128,128]{4,3,2,1,0:T(8,128)(2,1)} %param.9) | copy-start | bytes 4718596
  7.2 177.0 %reduce-scatter.3.cloned.1.call-start = ((), (), s32[]{:S(2)}) async-start(), calls=%async_computation.2 | async-start | bytes 1638400 | tf_op jit(solution)/shard_map/reduce_scatter | solution.py:48
  70.8 113.4 %copy-start.2 = (f32[64,256]{1,0:T(8,128)S(1)}, f32[64,256]{1,0:T(8,128)}, u32[]{:S(2)}) copy-start(f32[64,256]{1,0:T(8,128)} %param.10) | copy-start | bytes 196612
  70.8 415.6 %reduce-scatter.5.cloned.1.call-start = ((), (), s32[]{:S(2)}) async-start(), calls=%async_computation.3 | async-start | bytes 1081344 | tf_op jit(solution)/shard_map/reduce_scatter | solution.py:62
  322.4 40.3 %copy-start.1 = (f32[64,256]{1,0:T(8,128)}, f32[64,256]{1,0:T(8,128)S(1)}, u32[]{:S(2)}) copy-start(f32[64,256]{1,0:T(8,128)S(1)} %get-tuple-element.248) | copy-start | bytes 196612
  628.5 0.6 copy-start.3
Sparse Core Ops, SparseCore 0:
  70.9 87.8 reduce-scatter.2
  371.2 102.9 reduce-scatter.4
where the time goes:
time: 643 us; the launch traced here: 636 us
  blocking collectives  318 us (49%)
  local copies, waits for them, and re-layouts  136 us (21%)
  matrix products  110 us (17%)
  other arithmetic  54.5 us (8%)
  between operations  14.2 us (2%)
    psum x1, blocking collectives, shards(): lax.psum(jnp.dot(w_half, w_half.T, preferred_element_type=jnp.float32), (...  115 us
    psum x1, blocking collectives, shards(): lax.psum(jnp.dot(h_half, h_half.T, preferred_element_type=jnp.float32), (...  113 us
    dot_general x128, matrix products, update(): fitted = jnp.dot(gram_row, current, precision=lax.Precision.HIGHEST)  105 us
    dynamic_slice x128, local copies, waits for them, and re-layouts, update(): pivot = lax.dynamic_index_in_dim(gram_row, column, 0, keepdims=False)  80.6 us
    all_gather x1, blocking collectives, shards(): h_block = lax.all_gather(h_half, 'user', axis=1, tiled=True)  50.6 us
    dynamic_slice x64, local copies, waits for them, and re-layouts, update(): cross_row = lax.dynamic_index_in_dim(cross, column, 0, keepdims=False)  45.2 us
    max x64, other arithmetic, update(): new_row = jnp.maximum(old_row + (cross_row - fitted) / pivot, floor_value)  41.6 us
    all_gather x1, blocking collectives, shards(): w_block = lax.all_gather(w_half, 'item', axis=1, tiled=True)  39.3 us
  transfers between devices with their start and end apart: 2, of which 0 were waited for; matrix products, arithmetic and copies ran while one was open for 0% of the time, Pallas kernels for 0%

commit v1 on v0

v1 whole, which is shorter than its diff:
```python
import functools

import jax
import jax.numpy as jnp
from jax import lax
from jax.experimental import pallas as pl
from jax.experimental.pallas import tpu as pltpu
from jax.sharding import PartitionSpec as P

RANK = 64
TILE = 128
USER_TILES = 48
ITEM_TILES = 32
SLOTS = 48
NX, NYH, NC = 4, 4, 2
NYL, NZ = 2, 12
FLOOR = 0.0001
F32 = jnp.float32
BF16 = jnp.bfloat16
MESH = pl.DeviceIdType.MESH

ROW_SLOT, ROW_VALID, ROW_ITEM = 0, 48, 96
SLOT_ROW, SLOT_VALID, SLOT_PREV = 144, 192, 240
COL_LAST = 288


def place(user):
    return (user % 2) * 16 + user // 2


def table(tile_index):
    t = tile_index.reshape(SLOTS)
    valid = t >= 0
    row = jnp.where(valid, t // ITEM_TILES, -1)
    col = jnp.where(valid, t % ITEM_TILES, -1)
    slot = jnp.arange(SLOTS, dtype=jnp.int32)
    of_row = row[None, :] == jnp.arange(USER_TILES, dtype=jnp.int32)[:, None]
    row_slot = jnp.max(jnp.where(of_row, slot[None, :], 0), axis=1)
    row_valid = jnp.max(of_row.astype(jnp.int32), axis=1)
    row_item = jnp.max(jnp.where(of_row, place(jnp.maximum(col, 0))[None, :], 0), axis=1)
    before = (col[None, :] == col[:, None]) & (slot[None, :] < slot[:, None])
    prev = jnp.max(jnp.where(before, slot[None, :] + 1, 0), axis=1)
    of_col = col[None, :] == jnp.arange(ITEM_TILES, dtype=jnp.int32)[:, None]
    last = jnp.max(jnp.where(of_col, slot[None, :] + 1, 0), axis=1)
    return jnp.concatenate(
        [row_slot, row_valid, row_item, jnp.maximum(row, 0), valid.astype(jnp.int32), prev, last]
    )


def fold(gram):
    return jnp.concatenate([gram[:32, :], gram[32:, :]], axis=1)


def unfold(folded):
    return jnp.concatenate([folded[:, :64], folded[:, 64:]], axis=0)


def dot_t(a, b):
    return lax.dot_general(a, b, (((1,), (1,)), ((), ())), preferred_element_type=F32)


def hals(gram, start_ref, cross, spread, resid, out_ref):
    n = start_ref.shape[1]
    eye = lax.broadcasted_iota(jnp.int32, (RANK, RANK), 0) == lax.broadcasted_iota(
        jnp.int32, (RANK, RANK), 1
    )
    inverse = 1.0 / jnp.sum(jnp.where(eye, gram, 0.0), axis=1, keepdims=True)
    scaled = gram * inverse
    fitted = jnp.dot(gram, start_ref[...], precision=lax.Precision.HIGHEST, preferred_element_type=F32)
    resid[:, :n] = (cross - fitted) * inverse
    for k in range(RANK):
        spread[k] = jnp.broadcast_to(scaled[:, k : k + 1], (RANK, TILE))

    def block(b, _):
        at = pl.multiple_of(b * 8, 8)
        rows = pl.ds(at, 8)
        for lane in range(0, n, TILE):
            r = resid[rows, lane : lane + TILE]
            old = start_ref[rows, lane : lane + TILE]
            deltas = []
            news = []
            for i in range(8):
                new = jnp.maximum(old[i : i + 1] + r[i : i + 1], FLOOR)
                delta = jnp.broadcast_to(new - old[i : i + 1], (8, TILE))
                r = r - spread[b * 8 + i, rows, :] * delta
                deltas.append(delta)
                news.append(new)
            out_ref[rows, lane : lane + TILE] = jnp.concatenate(news, axis=0)
            for j in range(0, RANK, 8):
                acc = resid[j : j + 8, lane : lane + TILE]
                for i in range(8):
                    acc = acc - spread[b * 8 + i, j : j + 8, :] * deltas[i]
                resid[j : j + 8, lane : lane + TILE] = acc
        return 0

    lax.fori_loop(0, RANK // 8, block, 0)


def kernel(
    tab, vals, w_init, h_init, w_out, h_out,
    hbuf, wbuf, acc, ysend, yrecv, zsend, zrecv, gsend, grecv,
    csend, crecv, cgsend, cgrecv, xsend, xrecv, vsend, vrecv, own4, spread, resid,
    hy_s, hy_r, hx_s, hx_r, hc_s, hc_r, ya_s, ya_r, g_s, g_r, z_s, z_r,
    wz_s, wz_r, wy_s, wy_r, c_s, c_r, cg_s, cg_r, x_s, x_r, v_s, v_r,
):
    user = lax.axis_index("user")
    item = lax.axis_index("item")
    x, yh, core = user // 8, (user // 2) % 4, user % 2
    yl, z = item // NZ, item % NZ

    def at_user(x_, yh_, core_):
        return {"user": x_ * 8 + yh_ * 2 + core_, "item": item}

    def at_item(yl_, z_):
        return {"user": user, "item": yl_ * NZ + z_}

    to_y = [at_user(x, (yh + d) % 4, core) for d in range(1, 4)]
    to_x = [at_user((x + d) % 4, yh, core) for d in range(1, 4)]
    to_core = at_user(x, yh, 1 - core)
    to_yl = at_item(1 - yl, z)
    to_z = [at_item(yl, (z + d) % NZ) for d in range(1, NZ)]

    barrier = pltpu.get_barrier_semaphore()
    partners = to_y + to_x + [to_core, to_yl] + to_z
    for partner in partners:
        pl.semaphore_signal(barrier, inc=1, device_id=partner, device_id_type=MESH)
    mine = core * 16 + x * 4 + yh
    hbuf[mine] = h_init[...].astype(BF16)
    acc[0] = jnp.zeros((RANK, TILE), F32)
    pl.semaphore_wait(barrier, len(partners))

    sent = []

    def send(src, dst, s_sem, r_sem, device):
        copy = pltpu.make_async_remote_copy(
            src_ref=src, dst_ref=dst, send_sem=s_sem, recv_sem=r_sem, device_id=device, device_id_type=MESH
        )
        copy.start()
        sent.append(copy)
        return copy

    ys = [send(hbuf.at[mine], hbuf.at[mine], hy_s.at[d], hy_r.at[d], to_y[d]) for d in range(3)]
    for copy in ys:
        copy.wait_recv()
    line = pl.ds(core * 16 + x * 4, 4)
    xs = [send(hbuf.at[line], hbuf.at[line], hx_s.at[d], hx_r.at[d], to_x[d]) for d in range(3)]
    for copy in xs:
        copy.wait_recv()
    side = pl.ds(core * 16, 16)
    send(hbuf.at[side], hbuf.at[side], hc_s.at[0], hc_r.at[0], to_core).wait_recv()

    def gram_h(p, total):
        for q in range(4):
            part = hbuf[p * 4 + q]
            total = total + dot_t(part, part)
        return total

    gram = fold(lax.fori_loop(0, 8, gram_h, jnp.zeros((RANK, RANK), F32)))
    gsend[...] = gram
    g_copy = send(gsend, grecv, g_s.at[0], g_r.at[0], to_yl)

    def product(row):
        slot = tab[ROW_SLOT + row]
        weight = tab[ROW_VALID + row].astype(F32)
        return dot_t(hbuf[tab[ROW_ITEM + row]], vals[slot]) * weight

    y_copies = []
    for d in range(NZ):
        row = 2 * ((1 - yl) * NZ + (z + d) % NZ)
        ysend[d, :TILE // 2, :] = product(row).astype(BF16)
        ysend[d, TILE // 2 :, :] = product(row + 1).astype(BF16)
        y_copies.append(send(ysend.at[d], yrecv.at[d], ya_s.at[d], ya_r.at[d], to_yl))
    g_copy.wait_recv()
    gram = gram + grecv[...]
    gram_half = gram.astype(BF16)
    z_copies = []
    for d in list(range(1, NZ)) + [0]:
        row = 2 * (yl * NZ + (z + d) % NZ)
        first = product(row)
        second = product(row + 1)
        y_copies[d].wait_recv()
        first = first + yrecv[d, : TILE // 2, :].astype(F32)
        second = second + yrecv[d, TILE // 2 :, :].astype(F32)
        if d:
            zsend[d, :64, :] = first.astype(BF16)
            zsend[d, 64:128, :] = second.astype(BF16)
            zsend[d, 128:160, :] = gram_half
            z_copies.append(send(zsend.at[d], zrecv.at[d], z_s.at[d], z_r.at[d], to_z[d - 1]))
    for d in range(1, NZ):
        z_copies[d - 1].wait_recv()
        first = first + zrecv[d, :64, :].astype(F32)
        second = second + zrecv[d, 64:128, :].astype(F32)
        gram = gram + zrecv[d, 128:160, :].astype(F32)

    hals(unfold(gram), w_init, jnp.concatenate([first, second], axis=1), spread, resid, w_out)

    here = 2 * item
    wbuf[here] = w_out[:, :TILE].astype(BF16)
    wbuf[here + 1] = w_out[:, TILE:].astype(BF16)
    pair = pl.ds(here, 2)
    wz = [send(wbuf.at[pair], wbuf.at[pair], wz_s.at[d], wz_r.at[d], to_z[d - 1]) for d in range(1, NZ)]
    wy = [send(wbuf.at[pair], wbuf.at[pair], wy_s.at[0], wy_r.at[0], to_yl)]
    for d in range(1, NZ):
        wz[d - 1].wait_recv()
        came = pl.ds(2 * (yl * NZ + (z + NZ - d) % NZ), 2)
        wy.append(send(wbuf.at[came], wbuf.at[came], wy_s.at[d], wy_r.at[d], to_yl))
    for copy in wy:
        copy.wait_recv()

    def gram_w(p, total):
        for q in range(4):
            part = wbuf[p * 4 + q]
            total = total + dot_t(part, part)
        return total

    gram = fold(lax.fori_loop(0, 12, gram_w, jnp.zeros((RANK, RANK), F32)))
    cgsend[...] = gram
    cg_copy = send(cgsend, cgrecv, cg_s.at[0], cg_r.at[0], to_core)

    def by_slot(g, _):
        for q in range(8):
            s = g * 8 + q
            part = jnp.dot(wbuf[tab[SLOT_ROW + s]], vals[s], preferred_element_type=F32)
            acc[s + 1] = acc[tab[SLOT_PREV + s]] + part * tab[SLOT_VALID + s].astype(F32)
        return 0

    lax.fori_loop(0, SLOTS // 8, by_slot, 0)

    c_copies = []
    for dx in range(4):
        x_ = (x + dx) % 4
        for y_ in range(4):
            csend[dx, y_] = acc[tab[COL_LAST + x_ * 8 + y_ * 2 + (1 - core)]]
        c_copies.append(send(csend.at[dx], crecv.at[dx], c_s.at[dx], c_r.at[dx], to_core))
    cg_copy.wait_recv()
    gram = gram + cgrecv[...]
    x_copies = []
    for dx in (1, 2, 3, 0):
        x_ = (x + dx) % 4
        c_copies[dx].wait_recv()
        for y_ in range(4):
            total = acc[tab[COL_LAST + x_ * 8 + y_ * 2 + core]] + crecv[dx, y_]
            if dx:
                xsend[dx - 1, y_ * 64 : y_ * 64 + 64, :] = total
            else:
                own4[y_] = total
        if dx:
            xsend[dx - 1, 256:288, :] = gram
            x_copies.append(
                send(xsend.at[dx - 1], xrecv.at[dx - 1], x_s.at[dx - 1], x_r.at[dx - 1], to_x[dx - 1])
            )
    for dx in range(3):
        x_copies[dx].wait_recv()
        for y_ in range(4):
            own4[y_] += xrecv[dx, y_ * 64 : y_ * 64 + 64, :]
        gram = gram + xrecv[dx, 256:288, :]
    v_copies = []
    for dy in range(1, 4):
        vsend[dy - 1, :64, :] = own4[(yh + dy) % 4]
        vsend[dy - 1, 64:96, :] = gram
        v_copies.append(
            send(vsend.at[dy - 1], vrecv.at[dy - 1], v_s.at[dy - 1], v_r.at[dy - 1], to_y[dy - 1])
        )
    cross = own4[yh]
    for dy in range(3):
        v_copies[dy].wait_recv()
        cross = cross + vrecv[dy, :64, :]
        gram = gram + vrecv[dy, 64:96, :]

    hals(unfold(gram), h_init, cross, spread, resid, h_out)
    for copy in sent:
        copy.wait_send()


def shards(tile_index, tile_values, w_init, h_init):
    dma = lambda n: pltpu.SemaphoreType.DMA((n,))
    vmem = pl.BlockSpec(memory_space=pltpu.VMEM)
    return pl.pallas_call(
        kernel,
        out_shape=(
            jax.ShapeDtypeStruct(w_init.shape, F32),
            jax.ShapeDtypeStruct(h_init.shape, F32),
        ),
        in_specs=[pl.BlockSpec(memory_space=pltpu.SMEM), vmem, vmem, vmem],
        out_specs=(vmem, vmem),
        scratch_shapes=[
            pltpu.VMEM((32, RANK, TILE), BF16),
            pltpu.VMEM((48, RANK, TILE), BF16),
            pltpu.VMEM((SLOTS + 1, RANK, TILE), F32),
            pltpu.VMEM((NZ, TILE, TILE), BF16),
            pltpu.VMEM((NZ, TILE, TILE), BF16),
            pltpu.VMEM((NZ, 160, TILE), BF16),
            pltpu.VMEM((NZ, 160, TILE), BF16),
            pltpu.VMEM((32, TILE), F32),
            pltpu.VMEM((32, TILE), F32),
            pltpu.VMEM((4, 4, RANK, TILE), F32),
            pltpu.VMEM((4, 4, RANK, TILE), F32),
            pltpu.VMEM((32, TILE), F32),
            pltpu.VMEM((32, TILE), F32),
            pltpu.VMEM((3, 288, TILE), F32),
            pltpu.VMEM((3, 288, TILE), F32),
            pltpu.VMEM((3, 96, TILE), F32),
            pltpu.VMEM((3, 96, TILE), F32),
            pltpu.VMEM((4, RANK, TILE), F32),
            pltpu.VMEM((RANK, RANK, TILE), F32),
            pltpu.VMEM((RANK, 2 * TILE), F32),
            dma(3), dma(3), dma(3), dma(3), dma(1), dma(1),
            dma(NZ), dma(NZ), dma(1), dma(1), dma(NZ), dma(NZ),
            dma(NZ), dma(NZ), dma(NZ), dma(NZ),
            dma(4), dma(4), dma(1), dma(1), dma(3), dma(3), dma(3), dma(3),
        ],
        compiler_params=pltpu.CompilerParams(
            collective_id=0, has_side_effects=True, vmem_limit_bytes=40 * 2**20
        ),
        name="hals_sweep",
    )(table(tile_index), tile_values[0, 0], w_init, h_init)


def solution(mesh):
    in_specs = (
        P("user", "item", None),
        P("user", "item", None, None, None),
        P(None, ("user", "item")),
        P(None, ("item", "user")),
    )
    out_specs = (P(None, ("user", "item")), P(None, ("item", "user")))
    return jax.shard_map(shards, mesh=mesh, in_specs=in_specs, out_specs=out_specs, check_vma=False)
```

time: 643 us -> 109 us (0.17); the launches traced: 636 us -> 109 us
  blocking collectives: 318 us -> 0 us
  local copies, waits for them, and re-layouts: 136 us -> 4.34 us
  matrix products: 110 us -> 0 us
  Pallas kernels: 0 us -> 103 us
  other arithmetic: 54.5 us -> 1.64 us
  between operations: 14.2 us -> 0.65 us
    psum x2 -> x0, blocking collectives: 228 us -> none  [the longest x1 115 us: shards(): lax.psum(jnp.dot(w_half, w_half.T, preferred_element_type=jnp.float32), (...]
    dynamic_slice x192 -> x0, local copies, waits for them, and re-layouts: 126 us -> none  [the longest x128 80.6 us: update(): pivot = lax.dynamic_index_in_dim(gram_row, column, 0, keepdims=False)]
    dot_general x132 -> x0, matrix products: 110 us -> none  [the longest x128 105 us: update(): fitted = jnp.dot(gram_row, current, precision=lax.Precision.HIGHEST)]
    pallas_call x0 -> x1, Pallas kernels: none -> 103 us  [shards(): pl.pallas_call(kernel, out_shape=(jax.ShapeDtypeStruct(w_init.shape, F32)...]
    all_gather x2 -> x0, blocking collectives: 89.9 us -> none  [the longest x1 50.6 us: shards(): h_block = lax.all_gather(h_half, 'user', axis=1, tiled=True)]
    max x64 -> x1, other arithmetic: 41.6 us -> 0.67 us  [table(): jnp.maximum(row, 0)]
    scatter-add x2 -> x0, other arithmetic: 10.9 us -> none  [the longest x1 5.44 us: shards(): jax.ops.segment_sum(products_h, tile_cols, num_segments=ITEM_TILES)]
  transfers between devices with their start and end apart: 2 -> 0, of which waited for: 0 -> 0; matrix products, arithmetic and copies ran while one was open for 0% -> 0% of each run, Pallas kernels for 0% -> 0%
where the time goes in v1:
time: 109 us
  Pallas kernels  103 us (94%)
  local copies, waits for them, and re-layouts  4.34 us (4%)
  other arithmetic  1.64 us (2%)
    pallas_call x1, Pallas kernels, shards(): pl.pallas_call(kernel, out_shape=(jax.ShapeDtypeStruct(w_init.shape, F32)...  103 us
    unnamed x8, local copies, waits for them, and re-layouts  4.25 us

profile of v1, /device:TPU:1, one launch (start us, length us, event | category | flops | bytes accessed | tf_op | source)
XLA Modules:
  0.0 109.2 jit_solution(14504712851531248066)
XLA Ops:
  0.6 0.7 fusion.5
  1.3 0.7 broadcast_maximum_fusion
  2.0 0.1 select_reduce_fusion.3
  2.1 0.2 select_reduce_fusion.1
  2.3 0.1 concatenate.3.tab
  2.4 0.0 copy-start
  2.4 1.4 %copy-done = bf16[1,1,48,128,128]{4,3,2,1,0:T(8,128)(2,1)S(1)} copy-done((bf16[1,1,48,128,128]{4,3,2,1,0:T(8,128)(2,1)S(1)}, bf16[1,1,48,128,128]{4,3,2,1,0:T(8,128)(2,1)}, u32[]{:S(2)}) %copy-start) | copy-done | bytes 1572888
  3.8 0.0 copy-start.1
  3.8 0.8 copy-done.1
  4.6 0.0 copy-start.2
  4.6 0.8 copy-done.2
  5.4 102.6 %hals_sweep.1 = (f32[64,256]{1,0:T(8,128)S(1)}, f32[64,128]{1,0:T(8,128)S(1)}) custom-call(s32[320]{0:T(512)S(1)} %concatenate.3.tab, bf16[48,128,128]{2,1,0:T(8,128)(2,1)S(1)} %bitcast.27, f32[64,256]{1,0:T(8,128)S(1)} %copy-done.1, f32[64,128]{1,0:T(8,128)S(1)} %copy-done.2), custom_call_target="tpu_custom_call" | custom-call | tf_op jit(solution)/shard_map/hals_sweep/pallas_call | solution.py:278
  107.9 0.6 copy.8
  108.6 0.6 copy.9
  (1 shorter events, 0.0 us)
Async XLA Ops:
  2.4 1.4 %copy-start = (bf16[1,1,48,128,128]{4,3,2,1,0:T(8,128)(2,1)S(1)}, bf16[1,1,48,128,128]{4,3,2,1,0:T(8,128)(2,1)}, u32[]{:S(2)}) copy-start(bf16[1,1,48,128,128]{4,3,2,1,0:T(8,128)(2,1)} %param.5) | copy-start | bytes 4718596
  3.8 0.8 copy-start.1
  4.6 0.8 copy-start.2

commit v2 on v0

v2 whole, which is shorter than its diff:
```python
import jax
import jax.numpy as jnp
from jax import lax
from jax.experimental import pallas as pl
from jax.experimental.pallas import tpu as pltpu
from jax.sharding import PartitionSpec as P

RANK = 64
TILE = 128
SLOTS = 48
NYL, NZ = 2, 12
FLOOR = 0.0001
F32 = jnp.float32
BF16 = jnp.bfloat16
I32 = jnp.int32
MESH = pl.DeviceIdType.MESH

Z_ORDER = (6, -5, 5, -4, 4, 2, -2, -3, 3, 1, -1, 0)
Z_RELAY = {6: 3, 5: 2, 4: 1, -5: -2, -4: -1}
W_NEAR = (3, -3, 2, -2, 1, -1)
W_FAR = (4, -4, 5, -5, 6)
W_ORDER = (
    tuple((0, -o) for o in (0,) + W_NEAR)
    + tuple((0, -o) for o in W_FAR)
    + tuple((1, -o) for o in (0,) + W_NEAR)
    + tuple((1, -o) for o in W_FAR)
)


def dot_t(a, b):
    return lax.dot_general(a, b, (((1,), (1,)), ((), ())), preferred_element_type=F32)


def fold(gram):
    return jnp.concatenate([gram[:32, :], gram[32:, :]], axis=1)


def unfold(folded):
    return jnp.concatenate([folded[:, :64], folded[:, 64:]], axis=0)


def hals(gram, start_ref, cross, spread, resid, out_ref):
    n = start_ref.shape[1]
    eye = lax.broadcasted_iota(I32, (RANK, RANK), 0) == lax.broadcasted_iota(I32, (RANK, RANK), 1)
    inverse = 1.0 / jnp.sum(jnp.where(eye, gram, 0.0), axis=1, keepdims=True)
    scaled = gram * inverse
    fitted = jnp.dot(gram, start_ref[...], precision=lax.Precision.HIGHEST, preferred_element_type=F32)
    resid[:, :n] = (cross - fitted) * inverse
    for k in range(RANK):
        spread[k] = jnp.broadcast_to(scaled[:, k : k + 1], (RANK, TILE))

    def block(b, _):
        rows = pl.ds(pl.multiple_of(b * 8, 8), 8)
        for lane in range(0, n, TILE):
            r = resid[rows, lane : lane + TILE]
            old = start_ref[rows, lane : lane + TILE]
            deltas = []
            news = []
            for i in range(8):
                new = jnp.maximum(old[i : i + 1] + r[i : i + 1], FLOOR)
                delta = jnp.broadcast_to(new - old[i : i + 1], (8, TILE))
                r = r - spread[b * 8 + i, rows, :] * delta
                deltas.append(delta)
                news.append(new)
            out_ref[rows, lane : lane + TILE] = jnp.concatenate(news, axis=0)
            for j in range(0, RANK, 8):
                acc = resid[j : j + 8, lane : lane + TILE]
                for i in range(8):
                    acc = acc - spread[b * 8 + i, j : j + 8, :] * deltas[i]
                resid[j : j + 8, lane : lane + TILE] = acc
        return 0

    lax.fori_loop(0, RANK // 8, block, 0)


def kernel(
    tidx, vals_in, w_in, h_in, w_out, h_out,
    vals, w_init, h_init, hbuf, wbuf, acc, ysend, yrecv, zsend, zrecv, gsend, grecv,
    csend, crecv, xsend, xrecv, vsend, vrecv, own4, gsum, ghalf, cgrecv, gxrecv, gyrecv,
    spread, resid, tabv, rows_tab, cols_tab,
    in_sem, hy_s, hy_r, hx_s, hx_r, hc_s, hc_r, ya_s, ya_r, g_s, g_r, z_s, z_r,
    wz_s, wz_r, wy_s, wy_r, c_s, c_r, cg_s, cg_r, gx_s, gx_r, gy_s, gy_r, gc_s, gc_r, x_s, x_r, v_s, v_r,
):
    user = lax.axis_index("user")
    item = lax.axis_index("item")
    x, yh, core = user // 8, (user // 2) % 4, user % 2
    yl, z = item // NZ, item % NZ

    def at_user(x_, yh_, core_):
        return {"user": x_ * 8 + yh_ * 2 + core_, "item": item}

    def z_at(o):
        return lax.rem(z + (o + NZ), NZ)

    to_y = {d: at_user(x, (yh + d) % 4, core) for d in (2, 1, 3)}
    to_x = {d: at_user((x + d) % 4, yh, core) for d in (2, 1, 3)}
    to_core = at_user(x, yh, 1 - core)
    to_yl = {"user": user, "item": (1 - yl) * NZ + z}
    to_z = {o: {"user": user, "item": yl * NZ + z_at(o)} for o in W_NEAR}

    h_copy = pltpu.make_async_copy(h_in, h_init, in_sem.at[0])
    h_copy.start()
    barrier = pltpu.get_barrier_semaphore()
    partners = [to_core, to_yl] + list(to_y.values()) + list(to_x.values()) + list(to_z.values())
    for partner in partners:
        pl.semaphore_signal(barrier, inc=1, device_id=partner, device_id_type=MESH)
    w_copy = pltpu.make_async_copy(w_in, w_init, in_sem.at[1])
    w_copy.start()
    v_copy = pltpu.make_async_copy(vals_in, vals, in_sem.at[2])
    v_copy.start()
    h_copy.wait()

    def spot(dx, dy):
        return core * 16 + ((x + 4 - dx) % 4) * 4 + (yh + 4 - dy) % 4

    mine = spot(0, 0)
    hbuf[mine] = h_init[...].astype(BF16)
    pl.semaphore_wait(barrier, len(partners))

    sent = []

    def send(src, dst, s_sem, r_sem, device):
        copy = pltpu.make_async_remote_copy(
            src_ref=src, dst_ref=dst, send_sem=s_sem, recv_sem=r_sem, device_id=device, device_id_type=MESH
        )
        copy.start()
        sent.append(copy)
        return copy

    def pass_h(at, s_sem, r_sem, device):
        return send(hbuf.at[at], hbuf.at[at], s_sem, r_sem, device)

    h_y = {d: pass_h(mine, hy_s.at[d - 1], hy_r.at[d - 1], to_y[d]) for d in (2, 1, 3)}
    h_x = {}
    h_c = {}

    def on_x(dy):
        at = spot(0, dy)
        for dx in (2, 1, 3):
            n = (dx - 1) * 4 + dy
            h_x[dx, dy] = pass_h(at, hx_s.at[n], hx_r.at[n], to_x[dx])
        h_c[0, dy] = pass_h(at, hc_s.at[dy], hc_r.at[dy], to_core)

    on_x(0)

    lane = lax.broadcasted_iota(I32, (8, TILE), 1)
    slot_of = jnp.zeros((8, TILE), I32)
    col_of = jnp.full((8, TILE), -1, I32)
    for s in range(SLOTS):
        tile = tidx[s]
        hit = lane == lax.shift_right_arithmetic(tile, 5)
        slot_of = jnp.where(hit, s, slot_of)
        col_of = jnp.where(hit, lax.bitwise_and(tile, 31), col_of)
    tabv[0, 0:8, :] = slot_of
    tabv[0, 8:16, :] = col_of
    rows_copy = pltpu.make_async_copy(tabv.at[0], rows_tab, in_sem.at[3])
    rows_copy.start()
    rows_copy.wait()

    def slot_at(row):
        return rows_tab[0, row]

    def col_at(row):
        return rows_tab[8, row]

    def chunk(far, o):
        return (1 - yl if far else yl) * NZ + z_at(o)

    order = [(2 * chunk(far, o) + half) for far, o in W_ORDER for half in (0, 1)]
    cols = [col_at(row) for row in order]
    placed = jnp.full((8, TILE), -1, I32)
    for p, col in enumerate(cols):
        placed = jnp.where(lane == p, col, placed)
    prev = jnp.zeros((8, TILE), I32)
    last = jnp.zeros((8, TILE), I32)
    for p, col in enumerate(cols):
        prev = jnp.where((placed == col) & (lane > p) & (placed >= 0), p + 1, prev)
        last = jnp.where(lane == col, p + 1, last)
    tabv[1, 0:8, :] = prev
    tabv[1, 8:16, :] = last
    cols_copy = pltpu.make_async_copy(tabv.at[1], cols_tab, in_sem.at[4])
    cols_copy.start()
    cols_copy.wait()

    acc[0] = jnp.zeros((RANK, TILE), F32)

    def self_dot(ref, spots):
        total = None
        for at in spots:
            part = ref[at]
            term = dot_t(part, part)
            total = term if total is None else total + term
        return total

    for dy in (1, 3, 2):
        h_y[dy].wait_recv()
        on_x(dy)
    gram = self_dot(hbuf, [spot(0, dy) for dy in range(4)])
    for dy in (0, 1, 3, 2):
        for dx in (1, 3, 2):
            h_x[dx, dy].wait_recv()
            n = dx * 4 + dy
            h_c[dx, dy] = pass_h(spot(dx, dy), hc_s.at[n], hc_r.at[n], to_core)
        gram = gram + self_dot(hbuf, [spot(dx, dy) for dx in (1, 3, 2)])

    def other(dx, dy):
        return lax.rem(spot(dx, dy) + 16, 32)

    v_copy.wait()
    for dy in (0, 1, 3, 2):
        for dx in (0, 1, 3, 2):
            h_c[dx, dy].wait_recv()
        gram = gram + self_dot(hbuf, [other(dx, dy) for dx in (0, 1, 3, 2)])
    gram = fold(gram)
    gsend[...] = gram
    g_copy = send(gsend, grecv, g_s.at[0], g_r.at[0], to_yl)

    def product(row):
        col = jnp.maximum(col_at(row), 0)
        weight = jnp.where(col_at(row) >= 0, 1.0, 0.0)
        item_at = lax.bitwise_and(col, 1) * 16 + lax.shift_right_logical(col, 1)
        return dot_t(hbuf[item_at], vals[slot_at(row)]) * weight

    y_copies = []
    for i, o in enumerate(Z_ORDER):
        row = 2 * chunk(1, o)
        ysend[i, : TILE // 2, :] = product(row).astype(BF16)
        ysend[i, TILE // 2 :, :] = product(row + 1).astype(BF16)
        y_copies.append(send(ysend.at[i], yrecv.at[i], ya_s.at[i], ya_r.at[i], to_yl))
    g_copy.wait_recv()
    gram = gram + grecv[...]
    gram_half = gram.astype(BF16)

    z_copies = {}
    at_of = {o: i for i, o in enumerate(Z_ORDER)}
    for i, o in enumerate(Z_ORDER):
        row = 2 * chunk(0, o)
        first = product(row)
        second = product(row + 1)
        y_copies[i].wait_recv()
        first = first + yrecv[i, :64, :].astype(F32)
        second = second + yrecv[i, 64:, :].astype(F32)
        if o == 0:
            break
        part_gram = gram
        if abs(o) == 3:
            for far in [f for f in Z_RELAY if f * o > 0]:
                z_copies[far].wait_recv()
                j = at_of[far]
                first = first + zrecv[j, :64, :].astype(F32)
                second = second + zrecv[j, 64:128, :].astype(F32)
                part_gram = part_gram + zrecv[j, 128:160, :].astype(F32)
        zsend[i, :64, :] = first.astype(BF16)
        zsend[i, 64:128, :] = second.astype(BF16)
        zsend[i, 128:160, :] = part_gram.astype(BF16) if abs(o) == 3 else gram_half
        z_copies[o] = send(zsend.at[i], zrecv.at[i], z_s.at[i], z_r.at[i], to_z[Z_RELAY.get(o, o)])
    for o in (2, -2, 1, -1, -3, 3):
        z_copies[o].wait_recv()
        j = at_of[o]
        first = first + zrecv[j, :64, :].astype(F32)
        second = second + zrecv[j, 64:128, :].astype(F32)
        gram = gram + zrecv[j, 128:160, :].astype(F32)

    w_copy.wait()
    hals(unfold(gram), w_init, jnp.concatenate([first, second], axis=1), spread, resid, w_out)

    here = 2 * item
    wbuf[here] = w_out[:, :TILE].astype(BF16)
    wbuf[here + 1] = w_out[:, TILE:].astype(BF16)

    def pass_w(o, s_sem, r_sem, device):
        rows = pl.ds(2 * chunk(0, o), 2)
        return send(wbuf.at[rows], wbuf.at[rows], s_sem, r_sem, device)

    w_y = []

    def over(o):
        n = len(w_y)
        w_y.append(pass_w(o, wy_s.at[n], wy_r.at[n], to_yl))

    w_z = {o: pass_w(0, wz_s.at[n], wz_r.at[n], to_z[o]) for n, o in enumerate(W_NEAR)}
    over(0)
    for o in W_NEAR:
        w_z[o].wait_recv()
        if abs(o) == 3:
            for far in [f for f in W_FAR if f * o > 0]:
                n = 6 + W_FAR.index(far)
                w_z[far] = pass_w(-o, wz_s.at[n], wz_r.at[n], to_z[far - o])
        over(-o)

    gram_w = [jnp.zeros((RANK, RANK), F32)]

    def work(p):
        far, o = W_ORDER[p]
        for half in (0, 1):
            row = 2 * chunk(far, o) + half
            factors = wbuf[row]
            weight = jnp.where(col_at(row) >= 0, 1.0, 0.0)
            part = jnp.dot(factors, vals[slot_at(row)], preferred_element_type=F32) * weight
            acc[2 * p + half + 1] = acc[cols_tab[0, 2 * p + half]] + part
            gram_w[0] = gram_w[0] + dot_t(factors, factors)

    for p in range(7):
        work(p)
    for o in W_FAR:
        w_z[o].wait_recv()
        over(-o)
    for p in range(7, 12):
        work(p)
    for p in range(12, 24):
        w_y[p - 12].wait_recv()
        work(p)

    half_here = pl.ds(pl.multiple_of(core * 16, 16), 16)
    half_there = pl.ds(pl.multiple_of((1 - core) * 16, 16), 16)
    gsum[...] = fold(gram_w[0])
    cg_copy = send(gsum.at[half_there], cgrecv, cg_s.at[0], cg_r.at[0], to_core)

    def column(dx, dy, core_):
        return acc[cols_tab[8, ((x + dx) % 4) * 8 + ((yh + dy) % 4) * 2 + core_]]

    y_order = (2, 1, 3, 0)
    c_copies = {}
    for dy in y_order:
        for dx in range(4):
            csend[dy, dx] = column(dx, dy, 1 - core)
        c_copies[dy] = send(csend.at[dy], crecv.at[dy], c_s.at[dy], c_r.at[dy], to_core)
    cg_copy.wait_recv()
    half_sum = gsum[half_here, :] + cgrecv[...]
    ghalf[0] = half_sum
    gx = {d: send(ghalf.at[0], gxrecv.at[d - 1], gx_s.at[d - 1], gx_r.at[d - 1], to_x[d]) for d in (2, 1, 3)}
    x_copies = {}
    for dy in y_order:
        c_copies[dy].wait_recv()
        for dx in (2, 1, 3, 0):
            total = column(dx, dy, core) + crecv[dy, dx]
            if dx:
                n = (dx - 1) * 4 + dy
                xsend[n] = total
                x_copies[dx, dy] = send(xsend.at[n], xrecv.at[n], x_s.at[n], x_r.at[n], to_x[dx])
            else:
                own4[dy] = total
    for d in (1, 3, 2):
        gx[d].wait_recv()
        half_sum = half_sum + gxrecv[d - 1]
    ghalf[1] = half_sum
    gy = {d: send(ghalf.at[1], gyrecv.at[d - 1], gy_s.at[d - 1], gy_r.at[d - 1], to_y[d]) for d in (2, 1, 3)}
    v_copies = {}
    for dy in y_order:
        cross = own4[dy]
        for dx in (1, 3, 2):
            x_copies[dx, dy].wait_recv()
            cross = cross + xrecv[(dx - 1) * 4 + dy]
        if dy:
            vsend[dy - 1] = cross
            v_copies[dy] = send(vsend.at[dy - 1], vrecv.at[dy - 1], v_s.at[dy - 1], v_r.at[dy - 1], to_y[dy])
    for d in (1, 3, 2):
        gy[d].wait_recv()
        half_sum = half_sum + gyrecv[d - 1]
    ghalf[2] = half_sum
    gc = send(ghalf.at[2], ghalf.at[3], gc_s.at[0], gc_r.at[0], to_core)
    for d in (1, 3, 2):
        v_copies[d].wait_recv()
        cross = cross + vrecv[d - 1]
    gc.wait_recv()
    gsum_low = jnp.where(core == 0, half_sum, ghalf[3])
    gsum_high = jnp.where(core == 0, ghalf[3], half_sum)
    gram = jnp.concatenate([gsum_low, gsum_high], axis=0)

    hals(unfold(gram), h_init, cross, spread, resid, h_out)
    for copy in sent:
        copy.wait_send()


def shards(tile_index, tile_values, w_init, h_init):
    dma = lambda n: pltpu.SemaphoreType.DMA((n,))
    vmem = pl.BlockSpec(memory_space=pltpu.VMEM)
    hbm = pl.BlockSpec(memory_space=pl.ANY)
    return pl.pallas_call(
        kernel,
        out_shape=(
            jax.ShapeDtypeStruct(w_init.shape, F32),
            jax.ShapeDtypeStruct(h_init.shape, F32),
        ),
        in_specs=[pl.BlockSpec(memory_space=pltpu.SMEM), hbm, hbm, hbm],
        out_specs=(vmem, vmem),
        scratch_shapes=[
            pltpu.VMEM((SLOTS, TILE, TILE), BF16),
            pltpu.VMEM((RANK, 2 * TILE), F32),
            pltpu.VMEM((RANK, TILE), F32),
            pltpu.VMEM((32, RANK, TILE), BF16),
            pltpu.VMEM((48, RANK, TILE), BF16),
            pltpu.VMEM((SLOTS + 1, RANK, TILE), F32),
            pltpu.VMEM((NZ, TILE, TILE), BF16),
            pltpu.VMEM((NZ, TILE, TILE), BF16),
            pltpu.VMEM((NZ - 1, 160, TILE), BF16),
            pltpu.VMEM((NZ - 1, 160, TILE), BF16),
            pltpu.VMEM((32, TILE), F32),
            pltpu.VMEM((32, TILE), F32),
            pltpu.VMEM((4, 4, RANK, TILE), F32),
            pltpu.VMEM((4, 4, RANK, TILE), F32),
            pltpu.VMEM((12, RANK, TILE), F32),
            pltpu.VMEM((12, RANK, TILE), F32),
            pltpu.VMEM((3, RANK, TILE), F32),
            pltpu.VMEM((3, RANK, TILE), F32),
            pltpu.VMEM((4, RANK, TILE), F32),
            pltpu.VMEM((32, TILE), F32),
            pltpu.VMEM((4, 16, TILE), F32),
            pltpu.VMEM((16, TILE), F32),
            pltpu.VMEM((3, 16, TILE), F32),
            pltpu.VMEM((3, 16, TILE), F32),
            pltpu.VMEM((RANK, RANK, TILE), F32),
            pltpu.VMEM((RANK, 2 * TILE), F32),
            pltpu.VMEM((2, 16, TILE), I32),
            pltpu.SMEM((16, TILE), I32),
            pltpu.SMEM((16, TILE), I32),
            dma(5), dma(3), dma(3), dma(12), dma(12), dma(16), dma(16),
            dma(NZ), dma(NZ), dma(1), dma(1), dma(NZ - 1), dma(NZ - 1),
            dma(11), dma(11), dma(NZ), dma(NZ), dma(4), dma(4), dma(1), dma(1),
            dma(3), dma(3), dma(3), dma(3), dma(1), dma(1), dma(12), dma(12), dma(3), dma(3),
        ],
        compiler_params=pltpu.CompilerParams(
            collective_id=0, has_side_effects=True, vmem_limit_bytes=56 * 2**20
        ),
        name="hals_sweep",
    )(tile_index.reshape(SLOTS), tile_values[0, 0], w_init, h_init)


def solution(mesh):
    in_specs = (
        P("user", "item", None),
        P("user", "item", None, None, None),
        P(None, ("user", "item")),
        P(None, ("item", "user")),
    )
    out_specs = (P(None, ("user", "item")), P(None, ("item", "user")))
    return jax.shard_map(shards, mesh=mesh, in_specs=in_specs, out_specs=out_specs, check_vma=False)
```

time: 643 us -> 80.4 us (0.13); the launches traced: 636 us -> 80.1 us
  blocking collectives: 318 us -> 0 us
  local copies, waits for them, and re-layouts: 136 us -> 2.85 us
  matrix products: 110 us -> 0 us
  Pallas kernels: 0 us -> 76.6 us
  other arithmetic: 54.5 us -> 0 us
  between operations: 14.2 us -> 0.64 us
    psum x2 -> x0, blocking collectives: 228 us -> none  [the longest x1 115 us: shards(): lax.psum(jnp.dot(w_half, w_half.T, preferred_element_type=jnp.float32), (...]
    dynamic_slice x192 -> x0, local copies, waits for them, and re-layouts: 126 us -> none  [the longest x128 80.6 us: update(): pivot = lax.dynamic_index_in_dim(gram_row, column, 0, keepdims=False)]
    dot_general x132 -> x0, matrix products: 110 us -> none  [the longest x128 105 us: update(): fitted = jnp.dot(gram_row, current, precision=lax.Precision.HIGHEST)]
    all_gather x2 -> x0, blocking collectives: 89.9 us -> none  [the longest x1 50.6 us: shards(): h_block = lax.all_gather(h_half, 'user', axis=1, tiled=True)]
    pallas_call x0 -> x1, Pallas kernels: none -> 76.6 us  [shards(): pl.pallas_call(kernel, out_shape=(jax.ShapeDtypeStruct(w_init.shape, F32)...]
    max x64 -> x0, other arithmetic: 41.6 us -> none  [update(): new_row = jnp.maximum(old_row + (cross_row - fitted) / pivot, floor_value)]
    scatter-add x2 -> x0, other arithmetic: 10.9 us -> none  [the longest x1 5.44 us: shards(): jax.ops.segment_sum(products_h, tile_cols, num_segments=ITEM_TILES)]
  transfers between devices with their start and end apart: 2 -> 0, of which waited for: 0 -> 0; matrix products, arithmetic and copies ran while one was open for 0% -> 0% of each run, Pallas kernels for 0% -> 0%
where the time goes in v2:
time: 80.4 us; the launch traced here: 80.1 us
  Pallas kernels  76.6 us (95%)
  local copies, waits for them, and re-layouts  2.85 us (4%)
    pallas_call x1, Pallas kernels, shards(): pl.pallas_call(kernel, out_shape=(jax.ShapeDtypeStruct(w_init.shape, F32)...  76.6 us
    unnamed x2, local copies, waits for them, and re-layouts  2.85 us

profile of v2, /device:TPU:1, one launch (start us, length us, event | category | flops | bytes accessed | tf_op | source)
XLA Modules:
  0.0 80.1 jit_solution(5840033766219603436)
XLA Ops:
  0.6 76.6 %hals_sweep.1 = (f32[64,256]{1,0:T(8,128)}, f32[64,128]{1,0:T(8,128)}) custom-call(s32[48]{0:T(128)} %bitcast.3, bf16[48,128,128]{2,1,0:T(8,128)(2,1)} %bitcast.2, f32[64,256]{1,0:T(8,128)} %w_in.1, f32[64,128]{1,0:T(8,128)} %h_in.1), custom_call_target="tpu_custom_call" | custom-call | tf_op jit(solution)/shard_map/hals_sweep/pallas_call | solution.py:379
  77.3 1.5 %copy.8 = f32[64,256]{1,0:T(8,128)} copy(f32[64,256]{1,0:T(8,128)} %get-tuple-element.4) | data formatting | bytes 131072
  78.7 1.4 %copy.9 = f32[64,128]{1,0:T(8,128)} copy(f32[64,128]{1,0:T(8,128)} %get-tuple-element.5) | data formatting | bytes 65536

commit v3 on v2

v3 whole, which is shorter than its diff:
```python
import jax
import jax.numpy as jnp
from jax import lax
from jax.experimental import pallas as pl
from jax.experimental.pallas import tpu as pltpu
from jax.sharding import PartitionSpec as P

RANK = 64
TILE = 128
SLOTS = 48
NYL, NZ = 2, 12
FLOOR = 0.0001
F32 = jnp.float32
BF16 = jnp.bfloat16
I32 = jnp.int32
MESH = pl.DeviceIdType.MESH

Z_ORDER = (6, -5, 5, -4, 4, 2, -2, -3, 3, 1, -1, 0)
Z_RELAY = {6: 3, 5: 2, 4: 1, -5: -2, -4: -1}
W_NEAR = (3, -3, 2, -2, 1, -1)
W_FAR = (4, -4, 5, -5, 6)
W_ORDER = (
    tuple((0, -o) for o in (0,) + W_NEAR)
    + tuple((0, -o) for o in W_FAR)
    + tuple((1, -o) for o in (0,) + W_NEAR)
    + tuple((1, -o) for o in W_FAR)
)


def dot_t(a, b):
    return lax.dot_general(a, b, (((1,), (1,)), ((), ())), preferred_element_type=F32)


def fold(gram):
    return jnp.concatenate([gram[:32, :], gram[32:, :]], axis=1)


def unfold(folded):
    return jnp.concatenate([folded[:, :64], folded[:, 64:]], axis=0)


def hals(gram, start_ref, cross, out_ref):
    n = start_ref.shape[1]
    eye = lax.broadcasted_iota(I32, (RANK, RANK), 0) == lax.broadcasted_iota(I32, (RANK, RANK), 1)
    inverse = 1.0 / jnp.sum(jnp.where(eye, gram, 0.0), axis=1, keepdims=True)
    scaled = gram * inverse
    fitted = jnp.dot(gram, start_ref[...], precision=lax.Precision.HIGHEST, preferred_element_type=F32)
    whole = start_ref[...] + (cross - fitted) * inverse
    goal = [whole[j : j + 8, :] for j in range(0, RANK, 8)]
    for b in range(RANK // 8):
        old = start_ref[8 * b : 8 * b + 8, :]
        news = []
        for i in range(8):
            k = 8 * b + i
            new = jnp.maximum(goal[b][i : i + 1, :], FLOOR)
            delta = jnp.broadcast_to(new - old[i : i + 1, :], (8, n))
            for j in range(b, RANK // 8):
                goal[j] = goal[j] - jnp.broadcast_to(scaled[8 * j : 8 * j + 8, k : k + 1], (8, n)) * delta
            news.append(new)
        out_ref[8 * b : 8 * b + 8, :] = jnp.concatenate(news, axis=0)


def kernel(
    tidx, vals_in, w_in, h_in, w_out, h_out,
    vals, w_init, h_init, hbuf, wbuf, acc, ysend, yrecv, zsend, zrecv, gpart, gzrecv,
    csend, crecv, xsend, xrecv, vsend, vrecv, own4, gsum, gsum2, ghalf, cgrecv, gxrecv, gyrecv,
    tabv, rows_tab, cols_tab,
    in_sem, hy_s, hy_r, hx_s, hx_r, hc_s, hc_r, ya_s, ya_r, g_s, g_r, z_s, z_r,
    wz_s, wz_r, wy_s, wy_r, c_s, c_r, cg_s, cg_r, gx_s, gx_r, gy_s, gy_r, gc_s, gc_r, x_s, x_r, v_s, v_r,
):
    user = lax.axis_index("user")
    item = lax.axis_index("item")
    x, yh, core = user // 8, (user // 2) % 4, user % 2
    yl, z = item // NZ, item % NZ

    def at_user(x_, yh_, core_):
        return {"user": x_ * 8 + yh_ * 2 + core_, "item": item}

    def z_at(o):
        return lax.rem(z + (o + NZ), NZ)

    to_y = {d: at_user(x, (yh + d) % 4, core) for d in (2, 1, 3)}
    to_x = {d: at_user((x + d) % 4, yh, core) for d in (2, 1, 3)}
    to_core = at_user(x, yh, 1 - core)
    to_yl = {"user": user, "item": (1 - yl) * NZ + z}
    to_z = {o: {"user": user, "item": yl * NZ + z_at(o)} for o in W_NEAR}

    h_copy = pltpu.make_async_copy(h_in, h_init, in_sem.at[0])
    h_copy.start()
    barrier = pltpu.get_barrier_semaphore()
    partners = [to_y[2], to_z[3], to_z[-3], to_y[1], to_y[3], to_x[2], to_x[1], to_x[3], to_core]
    partners += [to_z[2], to_z[-2], to_z[1], to_z[-1], to_yl]
    for partner in partners:
        pl.semaphore_signal(barrier, inc=1, device_id=partner, device_id_type=MESH)
    w_copy = pltpu.make_async_copy(w_in, w_init, in_sem.at[1])
    w_copy.start()
    v_copy = pltpu.make_async_copy(vals_in, vals, in_sem.at[2])
    v_copy.start()
    h_copy.wait()

    def spot(dx, dy):
        return core * 16 + ((x + 4 - dx) % 4) * 4 + (yh + 4 - dy) % 4

    mine = spot(0, 0)
    hbuf[mine] = h_init[...].astype(BF16)
    lane = lax.broadcasted_iota(I32, (8, TILE), 1)
    slot_of = jnp.zeros((8, TILE), I32)
    col_of = jnp.full((8, TILE), -1, I32)
    for s in range(SLOTS):
        tile = tidx[s]
        hit = lane == lax.shift_right_arithmetic(tile, 5)
        slot_of = jnp.where(hit, s, slot_of)
        col_of = jnp.where(hit, lax.bitwise_and(tile, 31), col_of)
    tabv[0, 0:8, :] = slot_of
    tabv[0, 8:16, :] = col_of
    rows_copy = pltpu.make_async_copy(tabv.at[0], rows_tab, in_sem.at[3])
    rows_copy.start()
    pl.semaphore_wait(barrier, len(partners))

    sent = []

    def drain(keep=0):
        while len(sent) > keep:
            sent.pop(0).wait_send()


    def send(src, dst, s_sem, r_sem, device):
        copy = pltpu.make_async_remote_copy(
            src_ref=src, dst_ref=dst, send_sem=s_sem, recv_sem=r_sem, device_id=device, device_id_type=MESH
        )
        copy.start()
        sent.append(copy)
        return copy

    def pass_h(at, s_sem, r_sem, device):
        return send(hbuf.at[at], hbuf.at[at], s_sem, r_sem, device)

    h_y = {d: pass_h(mine, hy_s.at[d - 1], hy_r.at[d - 1], to_y[d]) for d in (2, 1, 3)}
    h_x = {}
    h_c = {}

    def on_x(dy):
        at = spot(0, dy)
        for dx in (2, 1, 3):
            n = (dx - 1) * 4 + dy
            h_x[dx, dy] = pass_h(at, hx_s.at[n], hx_r.at[n], to_x[dx])
        h_c[0, dy] = pass_h(at, hc_s.at[dy], hc_r.at[dy], to_core)

    on_x(0)

    acc[0] = jnp.zeros((RANK, TILE), F32)

    def self_dot(ref, spots):
        total = None
        for at in spots:
            part = ref[at]
            term = dot_t(part, part)
            total = term if total is None else total + term
        return total

    for dy in (1, 3, 2):
        h_y[dy].wait_recv()
        on_x(dy)

    rows_copy.wait()

    def slot_at(row):
        return rows_tab[0, row]

    def col_at(row):
        return rows_tab[8, row]

    def chunk(far, o):
        return (1 - yl if far else yl) * NZ + z_at(o)

    order = [(2 * chunk(far, o) + half) for far, o in W_ORDER for half in (0, 1)]
    cols = [col_at(row) for row in order]
    placed = jnp.full((8, TILE), -1, I32)
    for p, col in enumerate(cols):
        placed = jnp.where(lane == p, col, placed)
    prev = jnp.zeros((8, TILE), I32)
    last = jnp.zeros((8, TILE), I32)
    for p, col in enumerate(cols):
        prev = jnp.where((placed == col) & (lane > p) & (placed >= 0), p + 1, prev)
        last = jnp.where(lane == col, p + 1, last)
    tabv[1, 0:8, :] = prev
    tabv[1, 8:16, :] = last
    cols_copy = pltpu.make_async_copy(tabv.at[1], cols_tab, in_sem.at[4])
    cols_copy.start()

    gram = self_dot(hbuf, [spot(0, dy) for dy in range(4)])
    for dy in (0, 1, 3, 2):
        for dx in (1, 3, 2):
            h_x[dx, dy].wait_recv()
            n = dx * 4 + dy
            h_c[dx, dy] = pass_h(spot(dx, dy), hc_s.at[n], hc_r.at[n], to_core)
        gram = gram + self_dot(hbuf, [spot(dx, dy) for dx in (1, 3, 2)])

    def other(dx, dy):
        return lax.rem(spot(dx, dy) + 16, 32)

    v_copy.wait()
    cols_copy.wait()
    for dy in (0, 1, 3, 2):
        for dx in (0, 1, 3, 2):
            h_c[dx, dy].wait_recv()
        gram = gram + self_dot(hbuf, [other(dx, dy) for dx in (0, 1, 3, 2)])
    half_here = pl.ds(pl.multiple_of(core * 16, 16), 16)
    half_there = pl.ds(pl.multiple_of((1 - core) * 16, 16), 16)

    gsum[...] = fold(gram)
    part = gsum[half_here, :]
    gpart[0] = part
    at_of = {o: i for i, o in enumerate(Z_ORDER)}
    g_z = {}

    def pass_gram(o, n):
        i = at_of[o]
        g_z[o] = send(gpart.at[n], gzrecv.at[i], g_s.at[i], g_r.at[i], to_z[Z_RELAY.get(o, o)])

    def product(row):
        col = jnp.maximum(col_at(row), 0)
        weight = jnp.where(col_at(row) >= 0, 1.0, 0.0)
        item_at = lax.bitwise_and(col, 1) * 16 + lax.shift_right_logical(col, 1)
        return dot_t(hbuf[item_at], vals[slot_at(row)]) * weight

    y_copies = []
    for i, o in enumerate(Z_ORDER):
        row = 2 * chunk(1, o)
        ysend[i, : TILE // 2, :] = product(row).astype(BF16)
        ysend[i, TILE // 2 :, :] = product(row + 1).astype(BF16)
        y_copies.append(send(ysend.at[i], yrecv.at[i], ya_s.at[i], ya_r.at[i], to_yl))
        for o in ((6, -5, 5), (-4, 4, 2), (-2, 1, -1))[i] if i < 3 else ():
            pass_gram(o, 0)
    for o in (-3, 3):
        through = part
        for far in [f for f in Z_RELAY if Z_RELAY[f] * o > 0]:
            g_z[far].wait_recv()
            through = through + gzrecv[at_of[far]]
        gpart[1 if o > 0 else 2] = through
        pass_gram(o, 1 if o > 0 else 2)

    z_copies = {}

    def pass_z(o, lo, hi, n, device):
        i = at_of[o]
        rows = pl.ds(lo, hi - lo)
        return send(zsend.at[i, rows], zrecv.at[i, rows], z_s.at[n], z_r.at[n], device)

    def came(o, half):
        return zrecv[at_of[o], half * 64 : half * 64 + 64, :].astype(F32)

    for i, o in enumerate(Z_ORDER):
        row = 2 * chunk(0, o)
        first = product(row)
        second = product(row + 1)
        y_copies[i].wait_recv()
        first = first + yrecv[i, :64, :].astype(F32)
        second = second + yrecv[i, 64:, :].astype(F32)
        if o == 0:
            break
        if o == 3:
            z_copies[6].wait_recv()
            first = first + came(6, 0)
        if o == -3:
            z_copies[-6].wait_recv()
            second = second + came(6, 1)
        if abs(o) == 3:
            for far in [f for f in Z_RELAY if f * o > 0 and f != 6]:
                z_copies[far].wait_recv()
                first = first + came(far, 0)
                second = second + came(far, 1)
        zsend[i, :64, :] = first.astype(BF16)
        zsend[i, 64:, :] = second.astype(BF16)
        if o == 6:
            z_copies[6] = pass_z(6, 0, 64, i, to_z[3])
            z_copies[-6] = pass_z(6, 64, 128, NZ - 1, to_z[-3])
        else:
            z_copies[o] = pass_z(o, 0, 128, i, to_z[Z_RELAY.get(o, o)])
        if o == -2:
            for near in (2, -2, 1, -1, -3, 3):
                g_z[near].wait_recv()
                part = part + gzrecv[at_of[near]]
            gpart[3] = part
            g_yl = send(gpart.at[3], gpart.at[4], g_s.at[11], g_r.at[11], to_yl)
        if o == 1:
            g_yl.wait_recv()
            part = part + gpart[4]
            gpart[5] = part
            g_core = send(gpart.at[5], gpart.at[6], g_s.at[12], g_r.at[12], to_core)
    drain(25)
    for o in (2, -2, 1, -1, -3, 3):
        z_copies[o].wait_recv()
        first = first + came(o, 0)
        second = second + came(o, 1)
    g_core.wait_recv()

    def joined(here_, there_):
        return jnp.concatenate([jnp.where(core == 0, here_, there_), jnp.where(core == 0, there_, here_)], axis=0)

    gram = joined(part, gpart[6])

    w_copy.wait()
    hals(unfold(gram), w_init, jnp.concatenate([first, second], axis=1), w_out)

    here = 2 * item
    wbuf[here] = w_out[:, :TILE].astype(BF16)
    wbuf[here + 1] = w_out[:, TILE:].astype(BF16)

    def pass_w(o, s_sem, r_sem, device):
        rows = pl.ds(2 * chunk(0, o), 2)
        return send(wbuf.at[rows], wbuf.at[rows], s_sem, r_sem, device)

    w_y = []

    def over(o):
        n = len(w_y)
        w_y.append(pass_w(o, wy_s.at[n], wy_r.at[n], to_yl))

    over(0)
    w_z = {o: pass_w(0, wz_s.at[n], wz_r.at[n], to_z[o]) for n, o in enumerate(W_NEAR)}
    drain(7)
    for o in W_NEAR:
        w_z[o].wait_recv()
        if abs(o) == 3:
            half, n = (0, 10) if o > 0 else (1, 11)
            row = wbuf.at[2 * chunk(0, -o) + half]
            w_z[2 * o] = send(row, row, wz_s.at[n], wz_r.at[n], to_z[o])
            for far in [f for f in (5, -5, 4, -4) if f * o > 0]:
                n = 6 + W_FAR.index(far)
                w_z[far] = pass_w(-o, wz_s.at[n], wz_r.at[n], to_z[far - o])
        over(-o)

    gram_w = [jnp.zeros((RANK, RANK), F32)]

    def work(p):
        far, o = W_ORDER[p]
        for half in (0, 1):
            row = 2 * chunk(far, o) + half
            factors = wbuf[row]
            weight = jnp.where(col_at(row) >= 0, 1.0, 0.0)
            part = jnp.dot(factors, vals[slot_at(row)], preferred_element_type=F32) * weight
            acc[2 * p + half + 1] = acc[cols_tab[0, 2 * p + half]] + part
            gram_w[0] = gram_w[0] + dot_t(factors, factors)

    for p in range(7):
        work(p)
    for o in W_FAR:
        w_z[o].wait_recv()
        if o == 6:
            w_z[-6].wait_recv()
        over(-o)
    for p in range(7, 12):
        work(p)
    for p in range(12, 24):
        w_y[p - 12].wait_recv()
        work(p)

    gsum2[...] = fold(gram_w[0])
    cg_copy = send(gsum2.at[half_there], cgrecv, cg_s.at[0], cg_r.at[0], to_core)

    def column(dx, dy, core_):
        return acc[cols_tab[8, ((x + dx) % 4) * 8 + ((yh + dy) % 4) * 2 + core_]]

    y_order = (2, 1, 3, 0)
    c_copies = {}
    for dy in y_order:
        for dx in range(4):
            csend[dy, dx] = column(dx, dy, 1 - core)
        c_copies[dy] = send(csend.at[dy], crecv.at[dy], c_s.at[dy], c_r.at[dy], to_core)
    cg_copy.wait_recv()
    half_sum = gsum2[half_here, :] + cgrecv[...]
    ghalf[0] = half_sum
    gx = {d: send(ghalf.at[0], gxrecv.at[d - 1], gx_s.at[d - 1], gx_r.at[d - 1], to_x[d]) for d in (2, 1, 3)}
    x_copies = {}
    for dy in y_order:
        c_copies[dy].wait_recv()
        for dx in (2, 1, 3, 0):
            total = column(dx, dy, core) + crecv[dy, dx]
            if dx:
                n = (dx - 1) * 4 + dy
                xsend[n] = total
                x_copies[dx, dy] = send(xsend.at[n], xrecv.at[n], x_s.at[n], x_r.at[n], to_x[dx])
            else:
                own4[dy] = total
    drain(18)
    for d in (1, 3, 2):
        gx[d].wait_recv()
        half_sum = half_sum + gxrecv[d - 1]
    ghalf[1] = half_sum
    gy = {d: send(ghalf.at[1], gyrecv.at[d - 1], gy_s.at[d - 1], gy_r.at[d - 1], to_y[d]) for d in (2, 1, 3)}
    v_copies = {}
    for dy in y_order:
        cross = own4[dy]
        for dx in (1, 3, 2):
            x_copies[dx, dy].wait_recv()
            cross = cross + xrecv[(dx - 1) * 4 + dy]
        if dy:
            vsend[dy - 1] = cross
            v_copies[dy] = send(vsend.at[dy - 1], vrecv.at[dy - 1], v_s.at[dy - 1], v_r.at[dy - 1], to_y[dy])
    drain(6)
    for d in (1, 3, 2):
        gy[d].wait_recv()
        half_sum = half_sum + gyrecv[d - 1]
    ghalf[2] = half_sum
    gc = send(ghalf.at[2], ghalf.at[3], gc_s.at[0], gc_r.at[0], to_core)
    for d in (1, 3, 2):
        v_copies[d].wait_recv()
        cross = cross + vrecv[d - 1]
    gc.wait_recv()
    gram = joined(half_sum, ghalf[3])

    hals(unfold(gram), h_init, cross, h_out)
    drain()


def shards(tile_index, tile_values, w_init, h_init):
    dma = lambda n: pltpu.SemaphoreType.DMA((n,))
    vmem = pl.BlockSpec(memory_space=pltpu.VMEM)
    hbm = pl.BlockSpec(memory_space=pltpu.HBM)
    return pl.pallas_call(
        kernel,
        out_shape=(
            jax.ShapeDtypeStruct(w_init.shape, F32),
            jax.ShapeDtypeStruct(h_init.shape, F32),
        ),
        in_specs=[pl.BlockSpec(memory_space=pltpu.SMEM), hbm, hbm, hbm],
        out_specs=(vmem, vmem),
        scratch_shapes=[
            pltpu.VMEM((SLOTS, TILE, TILE), BF16),
            pltpu.VMEM((RANK, 2 * TILE), F32),
            pltpu.VMEM((RANK, TILE), F32),
            pltpu.VMEM((32, RANK, TILE), BF16),
            pltpu.VMEM((48, RANK, TILE), BF16),
            pltpu.VMEM((SLOTS + 1, RANK, TILE), F32),
            pltpu.VMEM((NZ, TILE, TILE), BF16),
            pltpu.VMEM((NZ, TILE, TILE), BF16),
            pltpu.VMEM((NZ - 1, TILE, TILE), BF16),
            pltpu.VMEM((NZ - 1, TILE, TILE), BF16),
            pltpu.VMEM((7, 16, TILE), F32),
            pltpu.VMEM((NZ - 1, 16, TILE), F32),
            pltpu.VMEM((4, 4, RANK, TILE), F32),
            pltpu.VMEM((4, 4, RANK, TILE), F32),
            pltpu.VMEM((12, RANK, TILE), F32),
            pltpu.VMEM((12, RANK, TILE), F32),
            pltpu.VMEM((3, RANK, TILE), F32),
            pltpu.VMEM((3, RANK, TILE), F32),
            pltpu.VMEM((4, RANK, TILE), F32),
            pltpu.VMEM((32, TILE), F32),
            pltpu.VMEM((32, TILE), F32),
            pltpu.VMEM((4, 16, TILE), F32),
            pltpu.VMEM((16, TILE), F32),
            pltpu.VMEM((3, 16, TILE), F32),
            pltpu.VMEM((3, 16, TILE), F32),
            pltpu.VMEM((2, 16, TILE), I32),
            pltpu.SMEM((16, TILE), I32),
            pltpu.SMEM((16, TILE), I32),
            dma(5), dma(3), dma(3), dma(12), dma(12), dma(16), dma(16),
            dma(NZ), dma(NZ), dma(13), dma(13), dma(NZ), dma(NZ),
            dma(NZ), dma(NZ), dma(NZ), dma(NZ), dma(4), dma(4), dma(1), dma(1),
            dma(3), dma(3), dma(3), dma(3), dma(1), dma(1), dma(12), dma(12), dma(3), dma(3),
        ],
        compiler_params=pltpu.CompilerParams(
            collective_id=0, has_side_effects=True, vmem_limit_bytes=20 * 2**20
        ),
        name="hals_sweep",
    )(
        tile_index.reshape(SLOTS),
        pltpu.with_memory_space_constraint(tile_values[0, 0], pltpu.HBM),
        pltpu.with_memory_space_constraint(w_init, pltpu.HBM),
        pltpu.with_memory_space_constraint(h_init, pltpu.HBM),
    )


def solution(mesh):
    in_specs = (
        P("user", "item", None),
        P("user", "item", None, None, None),
        P(None, ("user", "item")),
        P(None, ("item", "user")),
    )
    out_specs = (P(None, ("user", "item")), P(None, ("item", "user")))
    return jax.shard_map(shards, mesh=mesh, in_specs=in_specs, out_specs=out_specs, check_vma=False)
```

time: 80.4 us -> 76.9 us (0.956)
  Pallas kernels: 76.6 us -> 74.2 us
  local copies, waits for them, and re-layouts: 2.85 us -> 1.89 us
    pallas_call x1, Pallas kernels: 76.6 us -> 74.2 us  [shards(): pl.pallas_call(kernel, out_shape=(jax.ShapeDtypeStruct(w_init.shape, F32)...]
    unnamed x2 -> x4, local copies, waits for them, and re-layouts: 2.85 us -> 1.89 us
where the time goes in v3:
time: 76.9 us; the launch traced here: 76.7 us
  Pallas kernels  74.2 us (96%)
  local copies, waits for them, and re-layouts  1.89 us (2%)
    pallas_call x1, Pallas kernels, shards(): pl.pallas_call(kernel, out_shape=(jax.ShapeDtypeStruct(w_init.shape, F32)...  74.2 us
    unnamed x4, local copies, waits for them, and re-layouts  1.89 us

profile of v3, /device:TPU:1, one launch (start us, length us, event | category | flops | bytes accessed | tf_op | source)
XLA Modules:
  0.0 76.7 jit_solution(4810420058611647186)
XLA Ops:
  0.6 0.0 copy-start
  0.6 0.6 copy-done
  1.3 74.2 %hals_sweep.1 = (f32[64,256]{1,0:T(8,128)S(1)}, f32[64,128]{1,0:T(8,128)S(1)}) custom-call(s32[48]{0:T(128)S(1)} %bitcast.2, bf16[48,128,128]{2,1,0:T(8,128)(2,1)} %bitcast.3, f32[64,256]{1,0:T(8,128)} %w_in.1, f32[64,128]{1,0:T(8,128)} %h_in.1), custom_call_target="tpu_custom_call" | custom-call | tf_op jit(solution)/shard_map/hals_sweep/pallas_call | solution.py:421
  75.5 0.6 copy.8
  76.1 0.6 copy.9
Async XLA Ops:
  0.6 0.7 copy-start

commit v4 on v3

--- a/solution.py
+++ b/solution.py
@@ -232,14 +232,6 @@
         y_copies.append(send(ysend.at[i], yrecv.at[i], ya_s.at[i], ya_r.at[i], to_yl))
         for o in ((6, -5, 5), (-4, 4, 2), (-2, 1, -1))[i] if i < 3 else ():
             pass_gram(o, 0)
-    for o in (-3, 3):
-        through = part
-        for far in [f for f in Z_RELAY if Z_RELAY[f] * o > 0]:
-            g_z[far].wait_recv()
-            through = through + gzrecv[at_of[far]]
-        gpart[1 if o > 0 else 2] = through
-        pass_gram(o, 1 if o > 0 else 2)
-
     z_copies = {}
 
     def pass_z(o, lo, hi, n, device):
@@ -277,18 +269,25 @@
             z_copies[-6] = pass_z(6, 64, 128, NZ - 1, to_z[-3])
         else:
             z_copies[o] = pass_z(o, 0, 128, i, to_z[Z_RELAY.get(o, o)])
-        if o == -2:
+        if i == 3:
+            for side in (-3, 3):
+                through = part
+                for far in [f for f in Z_RELAY if Z_RELAY[f] * side > 0]:
+                    g_z[far].wait_recv()
+                    through = through + gzrecv[at_of[far]]
+                gpart[1 if side > 0 else 2] = through
+                pass_gram(side, 1 if side > 0 else 2)
+        if o == 1:
             for near in (2, -2, 1, -1, -3, 3):
                 g_z[near].wait_recv()
                 part = part + gzrecv[at_of[near]]
             gpart[3] = part
             g_yl = send(gpart.at[3], gpart.at[4], g_s.at[11], g_r.at[11], to_yl)
-        if o == 1:
-            g_yl.wait_recv()
-            part = part + gpart[4]
-            gpart[5] = part
-            g_core = send(gpart.at[5], gpart.at[6], g_s.at[12], g_r.at[12], to_core)
     drain(25)
+    g_yl.wait_recv()
+    part = part + gpart[4]
+    gpart[5] = part
+    g_core = send(gpart.at[5], gpart.at[6], g_s.at[12], g_r.at[12], to_core)
     for o in (2, -2, 1, -1, -3, 3):
         z_copies[o].wait_recv()
         first = first + came(o, 0)

time: 76.9 us -> 74.8 us (0.973)
  Pallas kernels: 74.2 us -> 72.1 us
    pallas_call x1, Pallas kernels: 74.2 us -> 72.1 us  [shards(): pl.pallas_call(kernel, out_shape=(jax.ShapeDtypeStruct(w_init.shape, F32)...]
where the time goes in v4:
time: 74.8 us; the launch traced here: 74.7 us
  Pallas kernels  72.1 us (96%)
  local copies, waits for them, and re-layouts  1.89 us (3%)
    pallas_call x1, Pallas kernels, shards(): pl.pallas_call(kernel, out_shape=(jax.ShapeDtypeStruct(w_init.shape, F32)...  72.1 us
    unnamed x4, local copies, waits for them, and re-layouts  1.89 us

profile of v4, /device:TPU:1, one launch (start us, length us, event | category | flops | bytes accessed | tf_op | source)
XLA Modules:
  0.0 74.7 jit_solution(10084896698381332493)
XLA Ops:
  0.6 0.0 copy-start
  0.6 0.6 copy-done
  1.3 72.1 %hals_sweep.1 = (f32[64,256]{1,0:T(8,128)S(1)}, f32[64,128]{1,0:T(8,128)S(1)}) custom-call(s32[48]{0:T(128)S(1)} %bitcast.2, bf16[48,128,128]{2,1,0:T(8,128)(2,1)} %bitcast.3, f32[64,256]{1,0:T(8,128)} %w_in.1, f32[64,128]{1,0:T(8,128)} %h_in.1), custom_call_target="tpu_custom_call" | custom-call | tf_op jit(solution)/shard_map/hals_sweep/pallas_call | solution.py:420
  73.4 0.6 copy.8
  74.1 0.6 copy.9
Async XLA Ops:
  0.6 0.7 copy-start

commit v5 on v4

--- a/solution.py
+++ b/solution.py
@@ -148,6 +148,15 @@
 
     on_x(0)
 
+    def slot_at(row):
+        return rows_tab[0, row]
+
+    def col_at(row):
+        return rows_tab[8, row]
+
+    def chunk(far, o):
+        return (1 - yl if far else yl) * NZ + z_at(o)
+
     acc[0] = jnp.zeros((RANK, TILE), F32)
 
     def self_dot(ref, spots):
@@ -162,17 +171,49 @@
         h_y[dy].wait_recv()
         on_x(dy)
 
+    for dy in (0, 1, 3, 2):
+        for dx in (1, 3, 2):
+            h_x[dx, dy].wait_recv()
+            n = dx * 4 + dy
+            h_c[dx, dy] = pass_h(spot(dx, dy), hc_s.at[n], hc_r.at[n], to_core)
+
+    def other(dx, dy):
+        return lax.rem(spot(dx, dy) + 16, 32)
+
+    gram = self_dot(hbuf, [spot(dx, dy) for dx in range(4) for dy in range(4)])
+    v_copy.wait()
     rows_copy.wait()
-
-    def slot_at(row):
-        return rows_tab[0, row]
-
-    def col_at(row):
-        return rows_tab[8, row]
-
-    def chunk(far, o):
-        return (1 - yl if far else yl) * NZ + z_at(o)
-
+    for dy in (0, 1, 3, 2):
+        for dx in (0, 1, 3, 2):
+            h_c[dx, dy].wait_recv()
+        gram = gram + self_dot(hbuf, [other(dx, dy) for dx in (0, 1, 3, 2)])
+    half_here = pl.ds(pl.multiple_of(core * 16, 16), 16)
+    half_there = pl.ds(pl.multiple_of((1 - core) * 16, 16), 16)
+
+    gsum[...] = fold(gram)
+    part = gsum[half_here, :]
+    gpart[0] = part
+    at_of = {o: i for i, o in enumerate(Z_ORDER)}
+    g_z = {}
+
+    def pass_gram(o, n):
+        i = at_of[o]
+        g_z[o] = send(gpart.at[n], gzrecv.at[i], g_s.at[i], g_r.at[i], to_z[Z_RELAY.get(o, o)])
+
+    def product(row):
+        col = jnp.maximum(col_at(row), 0)
+        weight = jnp.where(col_at(row) >= 0, 1.0, 0.0)
+        item_at = lax.bitwise_and(col, 1) * 16 + lax.shift_right_logical(col, 1)
+        return dot_t(hbuf[item_at], vals[slot_at(row)]) * weight
+
+    y_copies = []
+    for i, o in enumerate(Z_ORDER):
+        row = 2 * chunk(1, o)
+        ysend[i, : TILE // 2, :] = product(row).astype(BF16)
+        ysend[i, TILE // 2 :, :] = product(row + 1).astype(BF16)
+        y_copies.append(send(ysend.at[i], yrecv.at[i], ya_s.at[i], ya_r.at[i], to_yl))
+        for o in ((6, -5, 5), (-4, 4, 2), (-2, 1, -1))[i] if i < 3 else ():
+            pass_gram(o, 0)
     order = [(2 * chunk(far, o) + half) for far, o in W_ORDER for half in (0, 1)]
     cols = [col_at(row) for row in order]
     placed = jnp.full((8, TILE), -1, I32)
@@ -188,50 +229,6 @@
     cols_copy = pltpu.make_async_copy(tabv.at[1], cols_tab, in_sem.at[4])
     cols_copy.start()
 
-    gram = self_dot(hbuf, [spot(0, dy) for dy in range(4)])
-    for dy in (0, 1, 3, 2):
-        for dx in (1, 3, 2):
-            h_x[dx, dy].wait_recv()
-            n = dx * 4 + dy
-            h_c[dx, dy] = pass_h(spot(dx, dy), hc_s.at[n], hc_r.at[n], to_core)
-        gram = gram + self_dot(hbuf, [spot(dx, dy) for dx in (1, 3, 2)])
-
-    def other(dx, dy):
-        return lax.rem(spot(dx, dy) + 16, 32)
-
-    v_copy.wait()
-    cols_copy.wait()
-    for dy in (0, 1, 3, 2):
-        for dx in (0, 1, 3, 2):
-            h_c[dx, dy].wait_recv()
-        gram = gram + self_dot(hbuf, [other(dx, dy) for dx in (0, 1, 3, 2)])
-    half_here = pl.ds(pl.multiple_of(core * 16, 16), 16)
-    half_there = pl.ds(pl.multiple_of((1 - core) * 16, 16), 16)
-
-    gsum[...] = fold(gram)
-    part = gsum[half_here, :]
-    gpart[0] = part
-    at_of = {o: i for i, o in enumerate(Z_ORDER)}
-    g_z = {}
-
-    def pass_gram(o, n):
-        i = at_of[o]
-        g_z[o] = send(gpart.at[n], gzrecv.at[i], g_s.at[i], g_r.at[i], to_z[Z_RELAY.get(o, o)])
-
-    def product(row):
-        col = jnp.maximum(col_at(row), 0)
-        weight = jnp.where(col_at(row) >= 0, 1.0, 0.0)
-        item_at = lax.bitwise_and(col, 1) * 16 + lax.shift_right_logical(col, 1)
-        return dot_t(hbuf[item_at], vals[slot_at(row)]) * weight
-
-    y_copies = []
-    for i, o in enumerate(Z_ORDER):
-        row = 2 * chunk(1, o)
-        ysend[i, : TILE // 2, :] = product(row).astype(BF16)
-        ysend[i, TILE // 2 :, :] = product(row + 1).astype(BF16)
-        y_copies.append(send(ysend.at[i], yrecv.at[i], ya_s.at[i], ya_r.at[i], to_yl))
-        for o in ((6, -5, 5), (-4, 4, 2), (-2, 1, -1))[i] if i < 3 else ():
-            pass_gram(o, 0)
     z_copies = {}
 
     def pass_z(o, lo, hi, n, device):
@@ -330,6 +327,7 @@
                 w_z[far] = pass_w(-o, wz_s.at[n], wz_r.at[n], to_z[far - o])
         over(-o)
 
+    cols_copy.wait()
     gram_w = [jnp.zeros((RANK, RANK), F32)]
 
     def work(p):

time: 74.8 us -> 75.8 us (1.013)
  Pallas kernels: 72.1 us -> 73.1 us
    pallas_call x1, Pallas kernels: 72.1 us -> 73.1 us  [shards(): pl.pallas_call(kernel, out_shape=(jax.ShapeDtypeStruct(w_init.shape, F32)...]
where the time goes in v5:
time: 75.8 us; the launch traced here: 75.6 us
  Pallas kernels  73.1 us (96%)
  local copies, waits for them, and re-layouts  1.89 us (2%)
    pallas_call x1, Pallas kernels, shards(): pl.pallas_call(kernel, out_shape=(jax.ShapeDtypeStruct(w_init.shape, F32)...  73.1 us
    unnamed x4, local copies, waits for them, and re-layouts  1.89 us

profile of v5, /device:TPU:1, one launch (start us, length us, event | category | flops | bytes accessed | tf_op | source)
XLA Modules:
  0.0 75.6 jit_solution(13858914994734585232)
XLA Ops:
  0.6 0.0 copy-start
  0.6 0.6 copy-done
  1.3 73.1 %hals_sweep.1 = (f32[64,256]{1,0:T(8,128)S(1)}, f32[64,128]{1,0:T(8,128)S(1)}) custom-call(s32[48]{0:T(128)S(1)} %bitcast.2, bf16[48,128,128]{2,1,0:T(8,128)(2,1)} %bitcast.3, f32[64,256]{1,0:T(8,128)} %w_in.1, f32[64,128]{1,0:T(8,128)} %h_in.1), custom_call_target="tpu_custom_call" | custom-call | tf_op jit(solution)/shard_map/hals_sweep/pallas_call | solution.py:418
  74.4 0.6 copy.8
  75.0 0.6 copy.9
Async XLA Ops:
  0.6 0.7 copy-start
